TPU v7x, 512 devices: a whole 4x4x16 slice. The times are simulated.
512 devices in a mesh: dp: 16 (over x_hi, y, core), ctx: 32 (over x_lo, z).
Axes of the slice: x: 4 (x_hi: 2, x_lo: 2; x = x_hi * 2 + x_lo), y: 4, z: 16, core: 2. Of those that a mesh axis runs over, the one named last changes fastest.
Arguments:
- query: bfloat16 [16, 4096, 512], P('dp', 'ctx'), may hold values from -6 to 6
- key: bfloat16 [16, 4096, 512], P('dp', 'ctx'), may hold values from -6 to 6
- value: bfloat16 [16, 4096, 512], P('dp', 'ctx'), may hold values from -6 to 6
- out_grad: bfloat16 [16, 4096, 1024], P('dp', 'ctx'), may hold values from -6 to 6
- w_out: bfloat16 [512, 1024], P('dp'), may hold values from -0.25 to 0.25
- band_tiles: int32 [32, 3], replicated, may hold values from 0 to 1, as said below
- global_blocks: int32 [3], replicated, may hold values from 0 to 31, as said below
Outputs:
- query_grad: bfloat16 [16, 4096, 512], P('dp', 'ctx')
- key_grad: bfloat16 [16, 4096, 512], P('dp', 'ctx')
- value_grad: bfloat16 [16, 4096, 512], P('dp', 'ctx')
- w_out_grad: float32 [512, 1024], P(('dp', 'ctx'))
Inputs may be any that keep to these rules, and one draw needn't show every extreme that they name: band_tiles[a, c] = 1 lists the tile of query block a and key block a + c - 1; column 1 is 1 in every row; entries that point outside the utterance are ignored. `global_blocks`: distinct block numbers; 0 and 31 are among them.
All inputs are finite; a program needn't handle non-finite values.
Results may differ from a plain program's by a relative error of at most 0.03.
Values may be sent and summed in bfloat16 or wider, within the bound.
No kernel may reach another device: no remote copies, remote signals or barrier semaphores. Data moves between devices by JAX's collectives and lax.ppermute only.
A program may use at most 64 MiB of HBM per device.

v0:
```python
import jax
import jax.numpy as jnp
from jax import lax
from jax.sharding import PartitionSpec as P

HEADS = 4
HDIM = 128
BLK = 128


def padded(shard, sides, width):
    for axis, dim in sides:
        size, length = (lax.axis_size(axis), shard.shape[dim])
        up = [(i, (i + 1) % size) for i in range(size - 1)]
        down = [(j, i) for i, j in up]
        last = lax.slice_in_dim(shard, length - width, length, axis=dim)
        leading = lax.slice_in_dim(shard, 0, width, axis=dim)
        before = lax.ppermute(last, axis, up)
        after = lax.ppermute(leading, axis, down)
        shard = jnp.concatenate([before, shard, after], axis=dim)
    return shard


def from_behind(shard, axis, by):
    size = lax.axis_size(axis)
    pairs = [(i, i + by) for i in range(size) if 0 <= i + by < size]
    return lax.ppermute(shard, axis, pairs)


def tile_mask(band_tiles, global_blocks, q_first, q_count, k_first, k_count, n_blocks, band, blk):
    q_ids = q_first + jnp.arange(q_count, dtype=jnp.int32)
    k_ids = k_first + jnp.arange(k_count, dtype=jnp.int32)
    offset = k_ids[None, :] - q_ids[:, None]
    inside = (jnp.abs(offset) <= band) & (k_ids[None, :] >= 0) & (k_ids[None, :] < n_blocks)
    inside = inside & (q_ids[:, None] >= 0) & (q_ids[:, None] < n_blocks)
    table_hit = (q_ids[:, None] == jnp.arange(n_blocks, dtype=jnp.int32)[None, :]).astype(jnp.int32)
    rows_of = jnp.dot(table_hit, band_tiles)
    column = offset + band
    slots = jnp.arange(2 * band + 1, dtype=jnp.int32)
    chosen = jnp.sum(
        rows_of[:, None, :] * (column[:, :, None] == slots[None, None, :]).astype(jnp.int32), axis=2
    )
    shared = jnp.any(k_ids[:, None] == global_blocks[None, :], axis=1)
    tile = inside & (chosen > 0) & jnp.logical_not(shared)[None, :]
    full = jnp.broadcast_to(tile[:, None, :, None], (q_count, blk, k_count, blk))
    return full.reshape(q_count * blk, k_count * blk)


def contract_rows(left, right):
    return lax.dot_general(
        left, right, (((0,), (0,)), ((), ())), preferred_element_type=jnp.float32
    )


def contract_cols(left, right):
    return lax.dot_general(
        left, right, (((1,), (1,)), ((), ())), preferred_element_type=jnp.float32
    )


def on_device(query, key, value, out_grad, w_out, band_tiles, global_blocks):
    q_own = query[0]
    k_own = key[0]
    v_own = value[0]
    grad_own = out_grad[0]
    rows, width = q_own.shape
    per_dev = rows // BLK
    n_blocks = per_dev * lax.axis_size("ctx")
    first = lax.axis_index("ctx") * per_dev
    scale = HDIM ** (-0.5)
    d_out = contract_cols(grad_own, lax.all_gather(w_out, "dp", axis=0, tiled=True)).astype(
        jnp.bfloat16
    )
    pair = jnp.stack([k_own, v_own])
    wide = padded(pair, (("ctx", 1),), rows)
    local_ids = first + jnp.arange(per_dev, dtype=jnp.int32)
    pick = global_blocks[:, None] == local_ids[None, :]
    owned = jnp.einsum(
        "gb,cbrh->cgrh",
        pick.astype(jnp.bfloat16),
        pair.reshape(2, per_dev, BLK, width),
        preferred_element_type=jnp.float32,
    )
    shared = lax.psum(owned.astype(jnp.bfloat16), "ctx").reshape(2, -1, width)
    keys = jnp.concatenate([wide[0], shared[0]], 0)
    vals = jnp.concatenate([wide[1], shared[1]], 0)
    n_glob = shared.shape[1]
    band = tile_mask(
        band_tiles,
        global_blocks,
        first,
        per_dev,
        first - per_dev,
        3 * per_dev,
        n_blocks,
        per_dev,
        BLK,
    )
    mask = jnp.concatenate([band, jnp.ones((rows, n_glob), bool)], 1)
    outs, grads, key_parts, value_parts, maxima, totals, deltas = ([], [], [], [], [], [], [])
    for head in range(HEADS):
        low, high = (head * HDIM, (head + 1) * HDIM)
        q_head = q_own[:, low:high]
        k_head = keys[:, low:high]
        v_head = vals[:, low:high]
        d_head = d_out[:, low:high]
        scores = jnp.where(mask, contract_cols(q_head, k_head) * scale, -jnp.inf)
        peak = jnp.max(scores, axis=1, keepdims=True)
        expo = jnp.where(mask, jnp.exp(scores - peak), 0.0)
        total = jnp.sum(expo, axis=1, keepdims=True)
        prob = expo / total
        prob_low = prob.astype(jnp.bfloat16)
        out_head = jnp.dot(prob_low, v_head, preferred_element_type=jnp.float32).astype(
            jnp.bfloat16
        )
        delta = jnp.sum(
            d_head.astype(jnp.float32) * out_head.astype(jnp.float32), axis=1, keepdims=True
        )
        slope = contract_cols(d_head, v_head)
        dscore = (prob * (slope - delta)).astype(jnp.bfloat16)
        grads.append(
            (scale * jnp.dot(dscore, k_head, preferred_element_type=jnp.float32)).astype(
                jnp.bfloat16
            )
        )
        outs.append(out_head)
        maxima.append(peak)
        totals.append(total)
        deltas.append(delta)
        key_parts.append(scale * contract_rows(dscore, q_head))
        value_parts.append(contract_rows(prob_low, d_head))
    attended = jnp.concatenate(outs, 1)
    query_grad = jnp.concatenate(grads, 1)
    key_part = jnp.concatenate(key_parts, 1)
    value_part = jnp.concatenate(value_parts, 1)
    lower = jnp.stack([key_part[:rows], value_part[:rows]])
    upper = jnp.stack([key_part[2 * rows : 3 * rows], value_part[2 * rows : 3 * rows]])
    from_upper = from_behind(lower.astype(jnp.bfloat16), "ctx", -1).astype(lower.dtype)
    from_lower = from_behind(upper.astype(jnp.bfloat16), "ctx", 1).astype(upper.dtype)
    own = (
        jnp.stack([key_part[rows : 2 * rows], value_part[rows : 2 * rows]])
        + from_upper
        + from_lower
    )
    glob_part = jnp.stack([key_part[3 * rows :], value_part[3 * rows :]])
    glob_sum = (
        lax.psum(glob_part.astype(jnp.bfloat16), "ctx")
        .astype(jnp.float32)
        .reshape(2, -1, BLK, width)
    )
    back = jnp.einsum(
        "gb,cgrh->cbrh", pick.astype(jnp.float32), glob_sum, precision=lax.Precision.HIGHEST
    ).reshape(2, rows, width)
    summed = (own + back).astype(jnp.bfloat16)
    w_grad = lax.psum_scatter(
        contract_rows(attended, grad_own), ("dp", "ctx"), scatter_dimension=0, tiled=True
    )
    return (query_grad[None], summed[0][None], summed[1][None], w_grad)


def solution(mesh):
    return jax.shard_map(
        on_device,
        mesh=mesh,
        in_specs=(
            P("dp", "ctx", None),
            P("dp", "ctx", None),
            P("dp", "ctx", None),
            P("dp", "ctx", None),
            P("dp", None),
            P(),
            P(),
        ),
        out_specs=(
            P("dp", "ctx", None),
            P("dp", "ctx", None),
            P("dp", "ctx", None),
            P(("dp", "ctx"), None),
        ),
        check_vma=False,
    )
```

profile of v0, /device:TPU:1, one launch (start us, length us, event | category | flops | bytes accessed | tf_op | source)
XLA Modules:
  0.0 1029.6 jit_solution(11150613608643000979)
XLA Ops:
  10.7 1.1 fusion.18
  11.9 1.3 collective-permute-start.1
  13.2 5.0 collective-permute-start
  18.9 1.1 collective-permute-done.1
  20.0 1.5 collective-permute-done
  21.6 231.9 %all-reduce.6.cloned.1.call-done = bf16[2,3,128,512]{3,2,1,0:T(8,128)(2,1)} async-done(((bf16[2,3,128,512]{3,2,1,0:T(8,128)(2,1)}), bf16[2,3,128,512]{3,2,1,0:T(8,128)(2,1)}) %all-reduce.6.cloned.1.call-update) | async-done | bytes 786448 | tf_op jit(solution)/shard_map/psum | solution.py:84
  253.5 1.2 fusion.97
  256.7 1.0 convolution_convert_fusion.3
  257.7 1.0 convolution_convert_fusion.2
  258.7 1.0 convolution_convert_fusion.1
  259.8 1.7 convolution_convert_fusion
  264.0 1.0 multiply_reduce_fusion.3
  272.3 2.1 pad_maximum_fusion.3
  274.6 1.6 pad_maximum_fusion.5
  276.2 3.1 collective-permute-start.3
  279.5 1.3 pad_maximum_fusion
  280.8 1.8 fusion.30
  283.6 1.3 collective-permute-start.2
  284.9 1.0 slice_bitcast_fusion.5
  285.9 239.5 %all-reduce.8.cloned.1.call-done = bf16[2,3,128,512]{3,2,1,0:T(8,128)(2,1)} async-done(((bf16[2,3,128,512]{3,2,1,0:T(8,128)(2,1)}), bf16[2,3,128,512]{3,2,1,0:T(8,128)(2,1)}) %all-reduce.8.cloned.1.call-update) | async-done | bytes 786448 | tf_op jit(solution)/shard_map/psum | solution.py:147
  525.4 1.9 fusion.16
  527.3 1.1 fusion.21
  529.1 492.0 %all-reduce.10.cloned.1.call-done = f32[512,1024]{1,0:T(8,128)} async-done(((f32[512,1024]{1,0:T(8,128)}), f32[512,1024]{1,0:T(8,128)}) %all-reduce.10.cloned.1.call-update) | async-done | bytes 2097168
  1021.1 1.4 constant_dynamic-slice_fusion
  (130 shorter events, 17.0 us)
Async XLA Ops:
  8.0 251.8 %copy-start = (bf16[1,128,1024]{2,1,0:T(8,128)(2,1)S(1)}, bf16[1,128,1024]{2,1,0:T(8,128)(2,1)}, u32[]{:S(2)}) copy-start(bf16[1,128,1024]{2,1,0:T(8,128)(2,1)} %param.10) | copy-start | bytes 786436
  8.0 245.5 %all-reduce.6.cloned.1.call-start = ((), (), s32[]{:S(2)}) async-start(), calls=%async_computation | async-start | bytes 1572864 | tf_op jit(solution)/shard_map/psum | solution.py:84
  9.0 9.3 copy-start.34
  9.0 9.4 copy-start.24
  11.8 247.9 %all-gather.2.cloned.1.call-start = ((), (), s32[]{:S(2)}) async-start(), calls=%async_computation.1 | async-start | bytes 1114112 | tf_op jit(solution)/shard_map/all_gather | solution.py:71
  11.9 8.1 collective-permute-start.1
  13.2 8.3 collective-permute-start
  18.2 507.2 %all-reduce.8.cloned.1.call-start = ((), (), s32[]{:S(2)}) async-start(), calls=%async_computation.2 | async-start | bytes 1572864 | tf_op jit(solution)/shard_map/psum | solution.py:147
  21.6 236.1 %copy-start.9 = (bf16[384,512]{1,0:T(8,128)(2,1)}, bf16[384,512]{1,0:T(8,128)(2,1)S(1)}, u32[]{:S(2)}) copy-start(bf16[384,512]{1,0:T(8,128)(2,1)S(1)} %get-tuple-element.31) | copy-start | bytes 1179652
  21.6 233.2 %copy-start.13 = (bf16[1,128,512]{2,1,0:T(8,128)(2,1)S(1)}, bf16[1,128,512]{2,1,0:T(8,128)(2,1)}, u32[]{:S(2)}) copy-start(bf16[1,128,512]{2,1,0:T(8,128)(2,1)} %param.7) | copy-start | bytes 393220
  254.7 3.1 copy-start.11
  255.3 8.1 copy-start.3
  255.6 6.9 copy-start.5
  255.9 2.8 copy-start.25
  255.9 5.6 copy-start.7
  256.7 2.0 copy-start.32
  259.7 2.7 copy-start.31
  263.9 4.5 copy-start.1
  271.6 7.7 copy-start.2
  272.3 2.2 copy-start.16
  274.5 746.6 %all-reduce.10.cloned.1.call-start = ((), (), s32[]{:S(2)}) async-start(), calls=%async_computation.3 | async-start | bytes 4194304
  276.2 251.1 %collective-permute-start.3 = (bf16[2,128,512]{2,1,0:T(8,128)(2,1)}, bf16[2,128,512]{2,1,0:T(8,128)(2,1)}, u32[]{:S(2)}, u32[]{:S(2)}) collective-permute-start(bf16[2,128,512]{2,1,0:T(8,128)(2,1)} %pad_maximum_fusion.5), channel_id=1, source_target_pairs={{0,1},{1,2},{2,3},{3,4},{4,5},{5,6},{6,7},{7,8},{8,9},{9,10},{10,1... | collective-permute-start | bytes 786440 | tf_op jit(solution)/shard_map/ppermute | solution.py:27
  282.6 242.8 %copy-start.35 = (s32[3]{0:T(128)S(1)}, s32[3]{0:T(128)}, u32[]{:S(2)}) copy-start(s32[3]{0:T(128)} %param.13) | copy-start | bytes 40
  283.6 243.7 %collective-permute-start.2 = (bf16[2,128,512]{2,1,0:T(8,128)(2,1)S(1)}, bf16[2,128,512]{2,1,0:T(8,128)(2,1)S(1)}, u32[]{:S(2)}, u32[]{:S(2)}) collective-permute-start(bf16[2,128,512]{2,1,0:T(8,128)(2,1)S(1)} %pad_maximum_fusion.4), channel_id=1, source_target_pairs={{1,0},{2,1},{3,2},{4,3},{5,4},{6,5},{7,6},{8,7},{9,8},{10,9},{11,1... | collective-permute-start | bytes 786440 | tf_op jit(solution)/shard_map/ppermute | solution.py:27
  (20 other events, 24.1 us)
Sparse Core Ops, SparseCore 0:
  11.9 241.5 all-reduce.5
  274.6 250.7 all-reduce.7
  530.7 490.3 all-reduce.9
Sparse Core Ops, SparseCore 1:
  18.3 65.6 all-gather.1
where the time goes:
time: 1030 us
  waiting for transfers between devices  966 us (94%)
  between operations  15.8 us (2%)
  matrix products  15.2 us (1%)
  local copies, waits for them, and re-layouts  12.2 us (1%)
  starting transfers between devices  10.9 us (1%)
    unnamed x5, waiting for transfers between devices  492 us
    psum x1, waiting for transfers between devices, on_device(): lax.psum(glob_part.astype(jnp.bfloat16), 'ctx').astype(jnp.float32)  240 us
    psum x1, waiting for transfers between devices, on_device(): shared = lax.psum(owned.astype(jnp.bfloat16), 'ctx').reshape(2, -1, width)  232 us
  transfers between devices with their start and end apart: 8, of which 5 were waited for; matrix products, arithmetic and copies ran while one was open for 2% of the time, Pallas kernels for 0%

commit v1 on v0

--- a/solution.py
+++ b/solution.py
@@ -81,7 +81,9 @@
         pair.reshape(2, per_dev, BLK, width),
         preferred_element_type=jnp.float32,
     )
-    shared = lax.psum(owned.astype(jnp.bfloat16), "ctx").reshape(2, -1, width)
+    shared = jnp.sum(lax.all_gather(owned.astype(jnp.bfloat16), "ctx"), axis=0).reshape(
+        2, -1, width
+    )
     keys = jnp.concatenate([wide[0], shared[0]], 0)
     vals = jnp.concatenate([wide[1], shared[1]], 0)
     n_glob = shared.shape[1]

time: 1030 us -> 1130 us (1.097)
  waiting for transfers between devices: 966 us -> 1060 us
    all_gather x0 -> x1, waiting for transfers between devices: none -> 283 us  [on_device(): lax.all_gather(owned.astype(jnp.bfloat16), 'ctx')]
    psum x1 -> x0, waiting for transfers between devices: 232 us -> none  [on_device(): shared = lax.psum(owned.astype(jnp.bfloat16), 'ctx').reshape(2, -1, width)]
    all_gather x1, waiting for transfers between devices: 0.01 us -> 55.8 us  [on_device(): lax.all_gather(w_out, 'dp', axis=0, tiled=True)]
    psum x1, waiting for transfers between devices: 240 us -> 225 us  [on_device(): lax.psum(glob_part.astype(jnp.bfloat16), 'ctx').astype(jnp.float32)]
    reduce_sum x0 -> x1, other arithmetic: none -> 13 us  [on_device(): jnp.sum(lax.all_gather(owned.astype(jnp.bfloat16), 'ctx'), axis=0)]
  transfers between devices with their start and end apart: 8 -> 8, of which waited for: 5 -> 6; matrix products, arithmetic and copies ran while one was open for 2% -> 1% of each run, Pallas kernels for 0% -> 0%
where the time goes in v1:
time: 1130 us
  waiting for transfers between devices  1060 us (94%)
  other arithmetic  20.9 us (2%)
  between operations  14.2 us (1%)
  matrix products  12.6 us (1%)
    unnamed x5, waiting for transfers between devices  493 us
    all_gather x1, waiting for transfers between devices, on_device(): lax.all_gather(owned.astype(jnp.bfloat16), 'ctx')  283 us
    psum x1, waiting for transfers between devices, on_device(): lax.psum(glob_part.astype(jnp.bfloat16), 'ctx').astype(jnp.float32)  225 us
    all_gather x1, waiting for transfers between devices, on_device(): lax.all_gather(w_out, 'dp', axis=0, tiled=True)  55.8 us
  transfers between devices with their start and end apart: 8, of which 6 were waited for; matrix products, arithmetic and copies ran while one was open for 1% of the time, Pallas kernels for 0%

profile of v1, /device:TPU:1, one launch (start us, length us, event | category | flops | bytes accessed | tf_op | source)
XLA Modules:
  0.0 1127.8 jit_solution(4297355354902715088)
XLA Ops:
  8.0 0.9 constant_dynamic-update-slice_fusion.1
  8.9 0.9 constant_dynamic-update-slice_fusion
  10.6 1.1 fusion.18
  11.7 1.3 collective-permute-start.1
  13.0 5.0 collective-permute-start
  18.7 1.1 collective-permute-done.1
  19.8 1.5 collective-permute-done
  21.4 55.8 %all-gather.4.cloned.1.call-done = bf16[512,1024]{1,0:T(8,128)(2,1)} async-done(((bf16[32,1024]{1,0:T(8,128)(2,1)}), bf16[512,1024]{1,0:T(8,128)(2,1)}) %all-gather.4.cloned.1.call-update) | async-done | bytes 1048592 | tf_op jit(solution)/shard_map/all_gather | solution.py:71
  77.3 1.7 convolution_convert_fusion
  79.0 283.2 %all-gather.6.cloned.1.call-done = bf16[64,3,128,512]{3,2,1,0:T(8,128)(2,1)} async-done(((bf16[2,3,128,512]{3,2,1,0:T(8,128)(2,1)}), bf16[64,3,128,512]{3,2,1,0:T(8,128)(2,1)}) %all-gather.6.cloned.1.call-update) | async-done | bytes 25165840 | tf_op jit(solution)/shard_map/all_gather | solution.py:84
  362.2 13.0 %reduce_sum.94 = bf16[2,3,128,512]{3,2,1,0:T(8,128)(2,1)S(1)} reduce(bf16[32,2,3,128,512]{4,3,2,1,0:T(8,128)(2,1)} %bitcast.91, bf16[]{:T(256)} %constant.8.clone.1), dimensions={0}, to_apply=%region_2.0 | reduce | flops 12189696 | bytes 25952258 | tf_op jit(solution)/shard_map/reduce_sum | solution.py:84
  375.3 0.8 copy-done.3
  380.0 1.0 multiply_reduce_fusion.3
  388.3 2.1 pad_maximum_fusion.3
  390.5 1.6 pad_maximum_fusion.5
  392.1 2.0 collective-permute-start.3
  395.0 1.8 fusion.30
  396.8 0.9 copy-done.4
  397.8 1.3 collective-permute-start.2
  399.1 224.5 %all-reduce.5.cloned.1.call-done = bf16[2,3,128,512]{3,2,1,0:T(8,128)(2,1)} async-done(((bf16[2,3,128,512]{3,2,1,0:T(8,128)(2,1)}), bf16[2,3,128,512]{3,2,1,0:T(8,128)(2,1)}) %all-reduce.5.cloned.1.call-update) | async-done | bytes 786448 | tf_op jit(solution)/shard_map/psum | solution.py:149
  623.6 1.9 fusion.16
  625.6 1.1 fusion.21
  627.4 492.5 %all-reduce.7.cloned.1.call-done = f32[512,1024]{1,0:T(8,128)} async-done(((f32[512,1024]{1,0:T(8,128)}), f32[512,1024]{1,0:T(8,128)}) %all-reduce.7.cloned.1.call-update) | async-done | bytes 2097168
  1119.9 1.4 constant_dynamic-slice_fusion
  (91 shorter events, 15.0 us)
Async XLA Ops:
  7.2 70.1 %copy-start = (bf16[1,128,1024]{2,1,0:T(8,128)(2,1)S(1)}, bf16[1,128,1024]{2,1,0:T(8,128)(2,1)}, u32[]{:S(2)}) copy-start(bf16[1,128,1024]{2,1,0:T(8,128)(2,1)} %param.10) | copy-start | bytes 786436
  7.2 70.1 %all-gather.4.cloned.1.call-start = ((), (), s32[]{:S(2)}) async-start(), calls=%async_computation | async-start | bytes 1114112 | tf_op jit(solution)/shard_map/all_gather | solution.py:71
  7.9 354.3 %all-gather.6.cloned.1.call-start = ((), (), s32[]{:S(2)}) async-start(), calls=%async_computation.2 | async-start | bytes 25952256 | tf_op jit(solution)/shard_map/all_gather | solution.py:84
  8.9 9.2 copy-start.14
  8.9 9.5 copy-start.15
  11.7 611.9 %all-reduce.5.cloned.1.call-start = ((), (), s32[]{:S(2)}) async-start(), calls=%async_computation.1 | async-start | bytes 1572864 | tf_op jit(solution)/shard_map/psum | solution.py:149
  11.7 8.1 collective-permute-start.1
  13.0 8.3 collective-permute-start
  21.4 361.0 %copy-start.1 = (bf16[384,512]{1,0:T(8,128)(2,1)}, bf16[384,512]{1,0:T(8,128)(2,1)S(1)}, u32[]{:S(2)}) copy-start(bf16[384,512]{1,0:T(8,128)(2,1)S(1)} %get-tuple-element.31) | copy-start | bytes 1179652
  375.3 0.9 copy-start.3
  378.1 2.0 copy-start.7
  378.4 1.6 copy-start.9
  379.7 1.3 copy-start.11
  382.7 1.0 copy-start.2
  388.3 2.2 copy-start.6
  390.4 729.5 %all-reduce.7.cloned.1.call-start = ((), (), s32[]{:S(2)}) async-start(), calls=%async_computation.3 | async-start | bytes 4194304
  392.1 233.4 %collective-permute-start.3 = (bf16[2,128,512]{2,1,0:T(8,128)(2,1)}, bf16[2,128,512]{2,1,0:T(8,128)(2,1)}, u32[]{:S(2)}, u32[]{:S(2)}) collective-permute-start(bf16[2,128,512]{2,1,0:T(8,128)(2,1)} %pad_maximum_fusion.5), channel_id=1, source_target_pairs={{0,1},{1,2},{2,3},{3,4},{4,5},{5,6},{6,7},{7,8},{8,9},{9,10},{10,1... | collective-permute-start | bytes 786440 | tf_op jit(solution)/shard_map/ppermute | solution.py:27
  394.2 0.8 copy-start.8
  394.2 0.8 copy-start.10
  394.2 0.8 copy-start.12
  394.2 0.8 copy-start.13
  396.8 0.9 copy-start.4
  396.8 1.0 copy-start.5
  397.8 227.8 %collective-permute-start.2 = (bf16[2,128,512]{2,1,0:T(8,128)(2,1)S(1)}, bf16[2,128,512]{2,1,0:T(8,128)(2,1)S(1)}, u32[]{:S(2)}, u32[]{:S(2)}) collective-permute-start(bf16[2,128,512]{2,1,0:T(8,128)(2,1)S(1)} %pad_maximum_fusion.4), channel_id=1, source_target_pairs={{1,0},{2,1},{3,2},{4,3},{5,4},{6,5},{7,6},{8,7},{9,8},{10,9},{11,1... | collective-permute-start | bytes 786440 | tf_op jit(solution)/shard_map/ppermute | solution.py:27
Sparse Core Ops, SparseCore 0:
  11.4 65.8 all-gather.3
  79.4 282.8 all-gather.5
  390.5 233.0 all-reduce.4
  629.7 490.1 all-reduce.6
